TPU v7x, 32 devices: a whole 2x2x4 slice. The times are simulated.
32 devices in a mesh: gx: 8 (over y, x, core), gy: 4 (over z).
Axes of the slice: x: 2, y: 2, z: 4, core: 2. Of those that a mesh axis runs over, the one named last changes fastest.
Arguments:
- right_sides: bfloat16 [8, 4, 320, 1024], P('gx', 'gy'), may hold values from -2.5 to 2.5
- old_state: bfloat16 [8, 4, 320, 1024], P('gx', 'gy'), may hold values from -2.5 to 2.5
- plane_coupling: bfloat16 [8, 4, 2, 320, 320], P('gx', 'gy'), may hold values from -1.25 to 1.25
- face_coupling: bfloat16 [8, 4, 4, 320, 320], P('gx', 'gy'), may hold values from -0.25 to 0.25
- diag_inverse: bfloat16 [8, 4, 320, 320], P('gx', 'gy'), may hold values from -2 to 2
- neighbours: int32 [8, 4, 4], P('gx', 'gy'), may hold values from 0 to 2, as said below
Outputs:
- final_state: bfloat16 [8, 4, 320, 1024], P('gx', 'gy')
Inputs may be any that keep to these rules, and one draw needn't show every extreme that they name: `neighbours`: face 0 names one of the previous strip's elements (0 to 0), face 1 one of the next strip's (2 to 2); faces 2 and 3 may name any of the 3 candidates.
All inputs are finite; a program needn't handle non-finite values.
Results may differ from a plain program's by a relative error of at most 0.035.
Values may be sent and summed in bfloat16 or wider, within the bound.
A program may use at most 64 MiB of HBM per device.

v0:
```python
import jax
import jax.numpy as jnp
from jax import lax
from jax.sharding import PartitionSpec as P


def with_halo(shard, sides, width):
    for axis, dim in sides:
        peers, length = (lax.axis_size(axis), shard.shape[dim])
        up = [(i, (i + 1) % peers) for i in range(peers - 1)]
        down = [(j, i) for i, j in up]
        last = lax.slice_in_dim(shard, length - width, length, axis=dim)
        first = lax.slice_in_dim(shard, 0, width, axis=dim)
        before = lax.ppermute(last, axis, up)
        after = lax.ppermute(first, axis, down)
        shard = jnp.concatenate([before, shard, after], axis=dim)
    return shard


def from_behind(value, axis, steps):
    count = lax.axis_size(axis)
    first, last = (max(0, -steps), min(count, count - steps))
    return lax.ppermute(value, axis, [(source, source + steps) for source in range(first, last)])


def apply_block(blocks, states):
    return jnp.einsum("eij,ejr->eir", blocks, states, preferred_element_type=jnp.float32)


def gather_faces(state_pool, link_table, face_blocks):
    picked = jnp.take(state_pool, link_table.reshape(-1), axis=0)
    picked = picked.reshape(link_table.shape + state_pool.shape[1:])
    return jnp.einsum("efij,efjr->eir", face_blocks, picked, preferred_element_type=jnp.float32)


def sweep_chain(prepared, coupling, inverse, panels, backward, mover):
    elements, unknowns, columns = prepared.shape
    panel_width = columns // panels
    planes = lax.axis_size("gx")
    position = lax.axis_index("gx")
    turn_offset = planes - 1 - position if backward else position
    states = jnp.zeros(prepared.shape, jnp.bfloat16)
    products = jnp.zeros(prepared.shape, jnp.float32)
    carried = jnp.zeros((elements, unknowns, panel_width), jnp.bfloat16)

    def advance(turn_count, carry):
        states, products, carried = carry
        incoming = mover(carried)
        panel_index = turn_count - turn_offset
        active = (panel_index >= 0) & (panel_index < panels)
        panel_start = jnp.clip(panel_index, 0, panels - 1) * panel_width

        def compute(operands):
            states, products, incoming = operands
            coupled = apply_block(coupling, incoming)
            partial_sum = lax.dynamic_slice_in_dim(prepared, panel_start, panel_width, 2)
            residual = (partial_sum - coupled).astype(jnp.bfloat16)
            updated = apply_block(inverse, residual).astype(jnp.bfloat16)
            states = lax.dynamic_update_slice_in_dim(states, updated, panel_start, 2)
            products = lax.dynamic_update_slice_in_dim(products, coupled, panel_start, 2)
            return (states, products, updated)

        def passive(operands):
            states, products, incoming = operands
            return (states, products, jnp.zeros_like(incoming))

        return lax.cond(active, compute, passive, (states, products, incoming))

    states, products, carried = lax.fori_loop(
        0, planes + panels - 1, advance, (states, products, carried)
    )
    return (states, products)


def local(right_sides, old_state, plane_coupling, face_coupling, diag_inverse, neighbours):
    right_local = right_sides[0]
    old_local = old_state[0]
    lower_block = plane_coupling[0, :, 0]
    upper_block = plane_coupling[0, :, 1]
    face_local = face_coupling[0]
    inverse = diag_inverse[0]
    link_table = neighbours[0]
    panels = 4
    old_pool = with_halo(old_local, (("gy", 0),), old_local.shape[0])
    old_after = from_behind(old_local, "gx", -1)
    old_sum = (
        right_local
        - apply_block(upper_block, old_after)
        - gather_faces(old_pool, link_table, face_local)
    )

    def forward_mover(carried):
        return from_behind(carried, "gx", 1)

    half_state, lower_terms = sweep_chain(
        old_sum, lower_block, inverse, panels, False, forward_mover
    )
    half_pool = with_halo(half_state, (("gy", 0),), half_state.shape[0])
    half_sum = right_local - lower_terms - gather_faces(half_pool, link_table, face_local)

    def backward_mover(carried):
        return from_behind(carried, "gx", -1)

    final_state, unused = sweep_chain(half_sum, upper_block, inverse, panels, True, backward_mover)
    return final_state[None]


def solution(mesh):
    in_specs = (
        P("gx", "gy", None, None),
        P("gx", "gy", None, None),
        P("gx", "gy", None, None, None),
        P("gx", "gy", None, None, None),
        P("gx", "gy", None, None),
        P("gx", "gy", None),
    )
    out_specs = P("gx", "gy", None, None)
    return jax.shard_map(local, mesh=mesh, in_specs=in_specs, out_specs=out_specs, check_vma=False)
```

profile of v0, /device:TPU:3, one launch (start us, length us, event | category | flops | bytes accessed | tf_op | source)
XLA Modules:
  0.0 251.9 jit_solution(4737230339988109567)
XLA Ops:
  0.0 3.4 %collective-permute-start.3 = (bf16[1,320,1024]{2,1,0:T(8,128)(2,1)}, bf16[1,320,1024]{2,1,0:T(8,128)(2,1)S(1)}, u32[]{:S(2)}, u32[]{:S(2)}) collective-permute-start(bf16[1,320,1024]{2,1,0:T(8,128)(2,1)} %bitcast.112), channel_id=1, source_target_pairs={{0,1},{1,2},{2,3},{4,5},{5,6},{6,7},{8,9},{9,10},{10,11},{12,13},{... | collective-permute-start | bytes 1966088 | tf_op jit(solution)/shard_map/ppermute | solution.py:14
  4.7 2.9 %collective-permute-start.2 = (bf16[1,320,1024]{2,1,0:T(8,128)(2,1)}, bf16[1,320,1024]{2,1,0:T(8,128)(2,1)}, u32[]{:S(2)}, u32[]{:S(2)}) collective-permute-start(bf16[1,320,1024]{2,1,0:T(8,128)(2,1)} %bitcast.114), channel_id=1, source_target_pairs={{4,0},{8,4},{12,8},{16,12},{20,16},{24,20},{28,24},{5,1},{9,5},{13... | collective-permute-start | bytes 1966088 | tf_op jit(solution)/shard_map/ppermute | solution.py:23
  10.0 7.0 %collective-permute-done.3 = bf16[1,320,1024]{2,1,0:T(8,128)(2,1)S(1)} collective-permute-done((bf16[1,320,1024]{2,1,0:T(8,128)(2,1)}, bf16[1,320,1024]{2,1,0:T(8,128)(2,1)S(1)}, u32[]{:S(2)}, u32[]{:S(2)}) %collective-permute-start.3) | collective-permute-done | bytes 655392 | tf_op jit(solution)/shard_map/ppermute | solution.py:14
  17.9 3.0 %collective-permute-done.4 = bf16[1,320,1024]{2,1,0:T(8,128)(2,1)} collective-permute-done((bf16[1,320,1024]{2,1,0:T(8,128)(2,1)}, bf16[1,320,1024]{2,1,0:T(8,128)(2,1)}, u32[]{:S(2)}, u32[]{:S(2)}) %collective-permute-start.4) | collective-permute-done | bytes 655392 | tf_op jit(solution)/shard_map/ppermute | solution.py:15
  20.9 1.7 pad_maximum_fusion
  22.6 2.2 gather_fusion
  24.8 2.9 %fusion.24 = f32[320,1024]{1,0:T(8,128)S(1)} fusion(bf16[4,320,1024]{2,1,0:T(8,128)(2,1)} %gather_fusion, pred[4]{0:T(512)(128)(4,1)S(1)} %compare_and_fusion, bf16[1,1,4,320,320]{4,3,2,1,0:T(8,128)(2,1)S(1)} %copy-done), kind=kOutput, calls=%fused_computation.35 | convolution fusion | flops 840171520 | bytes 4751364 | tf_op jit(solution)/shard_map/efij,efjr->eir/dot_general | solution.py:33
  27.7 1.6 fusion.31
  32.2 97.4 %while.35 = (s32[]{:T(128)}, bf16[1,320,1024]{2,1,0:T(8,128)(2,1)}, f32[1,320,1024]{2,1,0:T(8,128)}, bf16[1,320,256]{2,1,0:T(8,128)(2,1)}, s32[]{:T(128)}, /*ind...) while((s32[]{:T(128)}, bf16[1,320,1024]{2,1,0:T(8,128)(2,1)}, ...), condition=%wide.region_3.5_spmd, body=%wide.region_0.4_spmd.sunk | while | flops 105103376 | bytes 2909541 | solution.py:69
  32.2 4.9 %collective-permute-start = (bf16[1,320,256]{2,1,0:T(8,128)(2,1)}, bf16[1,320,256]{2,1,0:T(8,128)(2,1)S(1)}, u32[]{:S(2)}, u32[]{:S(2)}) collective-permute-start(bf16[1,320,256]{2,1,0:T(8,128)(2,1)} %get-tuple-element.540), channel_id=1, source_target_pairs={{0,4},{4,8},{8,12},{12,16},{16,20},{20,24},{24,28},{1,5},{5,9},{9,... | collective-permute-start | bytes 491528 | tf_op jit(solution)/shard_map/while/body/eval_jaxpr/ppermute | solution.py:23
  37.0 2.5 %collective-permute-done = bf16[1,320,256]{2,1,0:T(8,128)(2,1)S(1)} collective-permute-done((bf16[1,320,256]{2,1,0:T(8,128)(2,1)}, bf16[1,320,256]{2,1,0:T(8,128)(2,1)S(1)}, u32[]{:S(2)}, u32[]{:S(2)}) %collective-permute-start) | collective-permute-done | bytes 163872 | tf_op jit(solution)/shard_map/while/body/eval_jaxpr/ppermute | solution.py:23
  40.2 5.2 %collective-permute-start = (bf16[1,320,256]{2,1,0:T(8,128)(2,1)}, bf16[1,320,256]{2,1,0:T(8,128)(2,1)S(1)}, u32[]{:S(2)}, u32[]{:S(2)}) collective-permute-start(bf16[1,320,256]{2,1,0:T(8,128)(2,1)} %get-tuple-element.540), channel_id=1, source_target_pairs={{0,4},{4,8},{8,12},{12,16},{16,20},{20,24},{24,28},{1,5},{5,9},{9,... | collective-permute-start | bytes 491528 | tf_op jit(solution)/shard_map/while/body/eval_jaxpr/ppermute | solution.py:23
  45.4 2.5 %collective-permute-done = bf16[1,320,256]{2,1,0:T(8,128)(2,1)S(1)} collective-permute-done((bf16[1,320,256]{2,1,0:T(8,128)(2,1)}, bf16[1,320,256]{2,1,0:T(8,128)(2,1)S(1)}, u32[]{:S(2)}, u32[]{:S(2)}) %collective-permute-start) | collective-permute-done | bytes 163872 | tf_op jit(solution)/shard_map/while/body/eval_jaxpr/ppermute | solution.py:23
  48.6 5.2 %collective-permute-start = (bf16[1,320,256]{2,1,0:T(8,128)(2,1)}, bf16[1,320,256]{2,1,0:T(8,128)(2,1)S(1)}, u32[]{:S(2)}, u32[]{:S(2)}) collective-permute-start(bf16[1,320,256]{2,1,0:T(8,128)(2,1)} %get-tuple-element.540), channel_id=1, source_target_pairs={{0,4},{4,8},{8,12},{12,16},{16,20},{20,24},{24,28},{1,5},{5,9},{9,... | collective-permute-start | bytes 491528 | tf_op jit(solution)/shard_map/while/body/eval_jaxpr/ppermute | solution.py:23
  53.8 2.5 %collective-permute-done = bf16[1,320,256]{2,1,0:T(8,128)(2,1)S(1)} collective-permute-done((bf16[1,320,256]{2,1,0:T(8,128)(2,1)}, bf16[1,320,256]{2,1,0:T(8,128)(2,1)S(1)}, u32[]{:S(2)}, u32[]{:S(2)}) %collective-permute-start) | collective-permute-done | bytes 163872 | tf_op jit(solution)/shard_map/while/body/eval_jaxpr/ppermute | solution.py:23
  57.0 5.2 %collective-permute-start = (bf16[1,320,256]{2,1,0:T(8,128)(2,1)}, bf16[1,320,256]{2,1,0:T(8,128)(2,1)S(1)}, u32[]{:S(2)}, u32[]{:S(2)}) collective-permute-start(bf16[1,320,256]{2,1,0:T(8,128)(2,1)} %get-tuple-element.540), channel_id=1, source_target_pairs={{0,4},{4,8},{8,12},{12,16},{16,20},{20,24},{24,28},{1,5},{5,9},{9,... | collective-permute-start | bytes 491528 | tf_op jit(solution)/shard_map/while/body/eval_jaxpr/ppermute | solution.py:23
  62.2 2.5 %collective-permute-done = bf16[1,320,256]{2,1,0:T(8,128)(2,1)S(1)} collective-permute-done((bf16[1,320,256]{2,1,0:T(8,128)(2,1)}, bf16[1,320,256]{2,1,0:T(8,128)(2,1)S(1)}, u32[]{:S(2)}, u32[]{:S(2)}) %collective-permute-start) | collective-permute-done | bytes 163872 | tf_op jit(solution)/shard_map/while/body/eval_jaxpr/ppermute | solution.py:23
  64.8 2.0 conditional.4
  66.7 3.9 %collective-permute-start = (bf16[1,320,256]{2,1,0:T(8,128)(2,1)}, bf16[1,320,256]{2,1,0:T(8,128)(2,1)S(1)}, u32[]{:S(2)}, u32[]{:S(2)}) collective-permute-start(bf16[1,320,256]{2,1,0:T(8,128)(2,1)} %get-tuple-element.540), channel_id=1, source_target_pairs={{0,4},{4,8},{8,12},{12,16},{16,20},{20,24},{24,28},{1,5},{5,9},{9,... | collective-permute-start | bytes 491528 | tf_op jit(solution)/shard_map/while/body/eval_jaxpr/ppermute | solution.py:23
  70.6 2.5 %collective-permute-done = bf16[1,320,256]{2,1,0:T(8,128)(2,1)S(1)} collective-permute-done((bf16[1,320,256]{2,1,0:T(8,128)(2,1)}, bf16[1,320,256]{2,1,0:T(8,128)(2,1)S(1)}, u32[]{:S(2)}, u32[]{:S(2)}) %collective-permute-start) | collective-permute-done | bytes 163872 | tf_op jit(solution)/shard_map/while/body/eval_jaxpr/ppermute | solution.py:23
  73.2 2.0 conditional.4
  75.2 5.1 %collective-permute-start = (bf16[1,320,256]{2,1,0:T(8,128)(2,1)}, bf16[1,320,256]{2,1,0:T(8,128)(2,1)S(1)}, u32[]{:S(2)}, u32[]{:S(2)}) collective-permute-start(bf16[1,320,256]{2,1,0:T(8,128)(2,1)} %get-tuple-element.540), channel_id=1, source_target_pairs={{0,4},{4,8},{8,12},{12,16},{16,20},{20,24},{24,28},{1,5},{5,9},{9,... | collective-permute-start | bytes 491528 | tf_op jit(solution)/shard_map/while/body/eval_jaxpr/ppermute | solution.py:23
  80.3 2.5 %collective-permute-done = bf16[1,320,256]{2,1,0:T(8,128)(2,1)S(1)} collective-permute-done((bf16[1,320,256]{2,1,0:T(8,128)(2,1)}, bf16[1,320,256]{2,1,0:T(8,128)(2,1)S(1)}, u32[]{:S(2)}, u32[]{:S(2)}) %collective-permute-start) | collective-permute-done | bytes 163872 | tf_op jit(solution)/shard_map/while/body/eval_jaxpr/ppermute | solution.py:23
  82.9 2.0 conditional.4
  84.8 5.2 %collective-permute-start = (bf16[1,320,256]{2,1,0:T(8,128)(2,1)}, bf16[1,320,256]{2,1,0:T(8,128)(2,1)S(1)}, u32[]{:S(2)}, u32[]{:S(2)}) collective-permute-start(bf16[1,320,256]{2,1,0:T(8,128)(2,1)} %get-tuple-element.540), channel_id=1, source_target_pairs={{0,4},{4,8},{8,12},{12,16},{16,20},{20,24},{24,28},{1,5},{5,9},{9,... | collective-permute-start | bytes 491528 | tf_op jit(solution)/shard_map/while/body/eval_jaxpr/ppermute | solution.py:23
  90.1 2.5 %collective-permute-done = bf16[1,320,256]{2,1,0:T(8,128)(2,1)S(1)} collective-permute-done((bf16[1,320,256]{2,1,0:T(8,128)(2,1)}, bf16[1,320,256]{2,1,0:T(8,128)(2,1)S(1)}, u32[]{:S(2)}, u32[]{:S(2)}) %collective-permute-start) | collective-permute-done | bytes 163872 | tf_op jit(solution)/shard_map/while/body/eval_jaxpr/ppermute | solution.py:23
  92.6 2.0 conditional.4
  94.6 5.1 %collective-permute-start = (bf16[1,320,256]{2,1,0:T(8,128)(2,1)}, bf16[1,320,256]{2,1,0:T(8,128)(2,1)S(1)}, u32[]{:S(2)}, u32[]{:S(2)}) collective-permute-start(bf16[1,320,256]{2,1,0:T(8,128)(2,1)} %get-tuple-element.540), channel_id=1, source_target_pairs={{0,4},{4,8},{8,12},{12,16},{16,20},{20,24},{24,28},{1,5},{5,9},{9,... | collective-permute-start | bytes 491528 | tf_op jit(solution)/shard_map/while/body/eval_jaxpr/ppermute | solution.py:23
  99.8 2.5 %collective-permute-done = bf16[1,320,256]{2,1,0:T(8,128)(2,1)S(1)} collective-permute-done((bf16[1,320,256]{2,1,0:T(8,128)(2,1)}, bf16[1,320,256]{2,1,0:T(8,128)(2,1)S(1)}, u32[]{:S(2)}, u32[]{:S(2)}) %collective-permute-start) | collective-permute-done | bytes 163872 | tf_op jit(solution)/shard_map/while/body/eval_jaxpr/ppermute | solution.py:23
  103.0 6.5 %collective-permute-start = (bf16[1,320,256]{2,1,0:T(8,128)(2,1)}, bf16[1,320,256]{2,1,0:T(8,128)(2,1)S(1)}, u32[]{:S(2)}, u32[]{:S(2)}) collective-permute-start(bf16[1,320,256]{2,1,0:T(8,128)(2,1)} %get-tuple-element.540), channel_id=1, source_target_pairs={{0,4},{4,8},{8,12},{12,16},{16,20},{20,24},{24,28},{1,5},{5,9},{9,... | collective-permute-start | bytes 491528 | tf_op jit(solution)/shard_map/while/body/eval_jaxpr/ppermute | solution.py:23
  109.5 2.5 %collective-permute-done = bf16[1,320,256]{2,1,0:T(8,128)(2,1)S(1)} collective-permute-done((bf16[1,320,256]{2,1,0:T(8,128)(2,1)}, bf16[1,320,256]{2,1,0:T(8,128)(2,1)S(1)}, u32[]{:S(2)}, u32[]{:S(2)}) %collective-permute-start) | collective-permute-done | bytes 163872 | tf_op jit(solution)/shard_map/while/body/eval_jaxpr/ppermute | solution.py:23
  112.7 5.2 %collective-permute-start = (bf16[1,320,256]{2,1,0:T(8,128)(2,1)}, bf16[1,320,256]{2,1,0:T(8,128)(2,1)S(1)}, u32[]{:S(2)}, u32[]{:S(2)}) collective-permute-start(bf16[1,320,256]{2,1,0:T(8,128)(2,1)} %get-tuple-element.540), channel_id=1, source_target_pairs={{0,4},{4,8},{8,12},{12,16},{16,20},{20,24},{24,28},{1,5},{5,9},{9,... | collective-permute-start | bytes 491528 | tf_op jit(solution)/shard_map/while/body/eval_jaxpr/ppermute | solution.py:23
  117.9 2.5 %collective-permute-done = bf16[1,320,256]{2,1,0:T(8,128)(2,1)S(1)} collective-permute-done((bf16[1,320,256]{2,1,0:T(8,128)(2,1)}, bf16[1,320,256]{2,1,0:T(8,128)(2,1)S(1)}, u32[]{:S(2)}, u32[]{:S(2)}) %collective-permute-start) | collective-permute-done | bytes 163872 | tf_op jit(solution)/shard_map/while/body/eval_jaxpr/ppermute | solution.py:23
  121.1 5.2 %collective-permute-start = (bf16[1,320,256]{2,1,0:T(8,128)(2,1)}, bf16[1,320,256]{2,1,0:T(8,128)(2,1)S(1)}, u32[]{:S(2)}, u32[]{:S(2)}) collective-permute-start(bf16[1,320,256]{2,1,0:T(8,128)(2,1)} %get-tuple-element.540), channel_id=1, source_target_pairs={{0,4},{4,8},{8,12},{12,16},{16,20},{20,24},{24,28},{1,5},{5,9},{9,... | collective-permute-start | bytes 491528 | tf_op jit(solution)/shard_map/while/body/eval_jaxpr/ppermute | solution.py:23
  126.3 2.5 %collective-permute-done = bf16[1,320,256]{2,1,0:T(8,128)(2,1)S(1)} collective-permute-done((bf16[1,320,256]{2,1,0:T(8,128)(2,1)}, bf16[1,320,256]{2,1,0:T(8,128)(2,1)S(1)}, u32[]{:S(2)}, u32[]{:S(2)}) %collective-permute-start) | collective-permute-done | bytes 163872 | tf_op jit(solution)/shard_map/while/body/eval_jaxpr/ppermute | solution.py:23
  129.5 3.2 %collective-permute-start.5 = (bf16[1,320,1024]{2,1,0:T(8,128)(2,1)}, bf16[1,320,1024]{2,1,0:T(8,128)(2,1)S(1)}, u32[]{:S(2)}, u32[]{:S(2)}) collective-permute-start(bf16[1,320,1024]{2,1,0:T(8,128)(2,1)} %get-tuple-element.374), channel_id=1, source_target_pairs={{0,1},{1,2},{2,3},{4,5},{5,6},{6,7},{8,9},{9,10},{10,11},{12,13},{... | collective-permute-start | bytes 1966088 | tf_op jit(solution)/shard_map/ppermute | solution.py:14
  134.0 9.9 %collective-permute-done.5 = bf16[1,320,1024]{2,1,0:T(8,128)(2,1)S(1)} collective-permute-done((bf16[1,320,1024]{2,1,0:T(8,128)(2,1)}, bf16[1,320,1024]{2,1,0:T(8,128)(2,1)S(1)}, u32[]{:S(2)}, u32[]{:S(2)}) %collective-permute-start.5) | collective-permute-done | bytes 655392 | tf_op jit(solution)/shard_map/ppermute | solution.py:14
  144.7 3.3 %collective-permute-done.6 = bf16[1,320,1024]{2,1,0:T(8,128)(2,1)} collective-permute-done((bf16[1,320,1024]{2,1,0:T(8,128)(2,1)}, bf16[1,320,1024]{2,1,0:T(8,128)(2,1)}, u32[]{:S(2)}, u32[]{:S(2)}) %collective-permute-start.6) | collective-permute-done | bytes 655392 | tf_op jit(solution)/shard_map/ppermute | solution.py:15
  148.0 1.7 pad_maximum_fusion.1
  149.7 2.2 gather_fusion.1
  151.9 3.4 %fusion.32 = f32[1,320,1024]{2,1,0:T(8,128)S(1)} fusion(bf16[4,320,1024]{2,1,0:T(8,128)(2,1)} %gather_fusion.1, pred[4]{0:T(512)(128)(4,1)S(1)} %compare_and_fusion, f32[1,320,1024]{2,1,0:T(8,128)} %get-tuple-element.373, bf16[1,1,320,1024]{3,2,1,0:T(8,128)(2,1)} %param.16, bf16[1,1,4,320,320]{4,3,2,1,0:T(8,128)(2,1)S(1)} %copy-done), kind=kOutput, calls=%fused_computation.40 | convolution fusion | flops 841154560 | bytes 6717444 | tf_op jit(solution)/shard_map/efij,efjr->eir/dot_general | solution.py:33
  156.9 95.0 %while.36 = (s32[]{:T(128)}, bf16[1,320,1024]{2,1,0:T(8,128)(2,1)}, bf16[1,320,256]{2,1,0:T(8,128)(2,1)}, s32[]{:T(128)}, f32[1,320,1024]{2,1,0:T(8,128)S(1)}, /...) while((s32[]{:T(128)}, bf16[1,320,1024]{2,1,0:T(8,128)(2,1)}, ...), condition=%wide.region_7.9_spmd, body=%wide.region_4.0_spmd.sunk | while | flops 105103376 | bytes 1967409 | solution.py:69
  156.9 1.9 collective-permute-start.1
  158.8 5.8 %collective-permute-done.1 = bf16[1,320,256]{2,1,0:T(8,128)(2,1)S(1)} collective-permute-done((bf16[1,320,256]{2,1,0:T(8,128)(2,1)}, bf16[1,320,256]{2,1,0:T(8,128)(2,1)S(1)}, u32[]{:S(2)}, u32[]{:S(2)}) %collective-permute-start.1) | collective-permute-done | bytes 163872 | tf_op jit(solution)/shard_map/while/body/eval_jaxpr/ppermute | solution.py:23
  165.3 1.9 collective-permute-start.1
  167.2 5.8 %collective-permute-done.1 = bf16[1,320,256]{2,1,0:T(8,128)(2,1)S(1)} collective-permute-done((bf16[1,320,256]{2,1,0:T(8,128)(2,1)}, bf16[1,320,256]{2,1,0:T(8,128)(2,1)S(1)}, u32[]{:S(2)}, u32[]{:S(2)}) %collective-permute-start.1) | collective-permute-done | bytes 163872 | tf_op jit(solution)/shard_map/while/body/eval_jaxpr/ppermute | solution.py:23
  173.7 1.9 collective-permute-start.1
  175.6 5.8 %collective-permute-done.1 = bf16[1,320,256]{2,1,0:T(8,128)(2,1)S(1)} collective-permute-done((bf16[1,320,256]{2,1,0:T(8,128)(2,1)}, bf16[1,320,256]{2,1,0:T(8,128)(2,1)S(1)}, u32[]{:S(2)}, u32[]{:S(2)}) %collective-permute-start.1) | collective-permute-done | bytes 163872 | tf_op jit(solution)/shard_map/while/body/eval_jaxpr/ppermute | solution.py:23
  182.1 1.9 collective-permute-start.1
  184.0 5.8 %collective-permute-done.1 = bf16[1,320,256]{2,1,0:T(8,128)(2,1)S(1)} collective-permute-done((bf16[1,320,256]{2,1,0:T(8,128)(2,1)}, bf16[1,320,256]{2,1,0:T(8,128)(2,1)S(1)}, u32[]{:S(2)}, u32[]{:S(2)}) %collective-permute-start.1) | collective-permute-done | bytes 163872 | tf_op jit(solution)/shard_map/while/body/eval_jaxpr/ppermute | solution.py:23
  190.5 1.9 collective-permute-start.1
  192.4 5.8 %collective-permute-done.1 = bf16[1,320,256]{2,1,0:T(8,128)(2,1)S(1)} collective-permute-done((bf16[1,320,256]{2,1,0:T(8,128)(2,1)}, bf16[1,320,256]{2,1,0:T(8,128)(2,1)S(1)}, u32[]{:S(2)}, u32[]{:S(2)}) %collective-permute-start.1) | collective-permute-done | bytes 163872 | tf_op jit(solution)/shard_map/while/body/eval_jaxpr/ppermute | solution.py:23
  199.5 1.9 collective-permute-start.1
  201.4 5.8 %collective-permute-done.1 = bf16[1,320,256]{2,1,0:T(8,128)(2,1)S(1)} collective-permute-done((bf16[1,320,256]{2,1,0:T(8,128)(2,1)}, bf16[1,320,256]{2,1,0:T(8,128)(2,1)S(1)}, u32[]{:S(2)}, u32[]{:S(2)}) %collective-permute-start.1) | collective-permute-done | bytes 163872 | tf_op jit(solution)/shard_map/while/body/eval_jaxpr/ppermute | solution.py:23
  208.6 1.9 collective-permute-start.1
  210.5 5.8 %collective-permute-done.1 = bf16[1,320,256]{2,1,0:T(8,128)(2,1)S(1)} collective-permute-done((bf16[1,320,256]{2,1,0:T(8,128)(2,1)}, bf16[1,320,256]{2,1,0:T(8,128)(2,1)S(1)}, u32[]{:S(2)}, u32[]{:S(2)}) %collective-permute-start.1) | collective-permute-done | bytes 163872 | tf_op jit(solution)/shard_map/while/body/eval_jaxpr/ppermute | solution.py:23
  217.6 1.9 collective-permute-start.1
  219.5 5.8 %collective-permute-done.1 = bf16[1,320,256]{2,1,0:T(8,128)(2,1)S(1)} collective-permute-done((bf16[1,320,256]{2,1,0:T(8,128)(2,1)}, bf16[1,320,256]{2,1,0:T(8,128)(2,1)S(1)}, u32[]{:S(2)}, u32[]{:S(2)}) %collective-permute-start.1) | collective-permute-done | bytes 163872 | tf_op jit(solution)/shard_map/while/body/eval_jaxpr/ppermute | solution.py:23
  226.6 1.9 collective-permute-start.1
  228.6 5.8 %collective-permute-done.1 = bf16[1,320,256]{2,1,0:T(8,128)(2,1)S(1)} collective-permute-done((bf16[1,320,256]{2,1,0:T(8,128)(2,1)}, bf16[1,320,256]{2,1,0:T(8,128)(2,1)S(1)}, u32[]{:S(2)}, u32[]{:S(2)}) %collective-permute-start.1) | collective-permute-done | bytes 163872 | tf_op jit(solution)/shard_map/while/body/eval_jaxpr/ppermute | solution.py:23
  235.0 1.9 collective-permute-start.1
  237.0 5.8 %collective-permute-done.1 = bf16[1,320,256]{2,1,0:T(8,128)(2,1)S(1)} collective-permute-done((bf16[1,320,256]{2,1,0:T(8,128)(2,1)}, bf16[1,320,256]{2,1,0:T(8,128)(2,1)S(1)}, u32[]{:S(2)}, u32[]{:S(2)}) %collective-permute-start.1) | collective-permute-done | bytes 163872 | tf_op jit(solution)/shard_map/while/body/eval_jaxpr/ppermute | solution.py:23
  243.5 1.9 collective-permute-start.1
  245.4 5.8 %collective-permute-done.1 = bf16[1,320,256]{2,1,0:T(8,128)(2,1)S(1)} collective-permute-done((bf16[1,320,256]{2,1,0:T(8,128)(2,1)}, bf16[1,320,256]{2,1,0:T(8,128)(2,1)S(1)}, u32[]{:S(2)}, u32[]{:S(2)}) %collective-permute-start.1) | collective-permute-done | bytes 163872 | tf_op jit(solution)/shard_map/while/body/eval_jaxpr/ppermute | solution.py:23
  (68 shorter events, 48.1 us)
Async XLA Ops:
  0.0 24.8 %copy-start = (bf16[1,1,4,320,320]{4,3,2,1,0:T(8,128)(2,1)S(1)}, bf16[1,1,4,320,320]{4,3,2,1,0:T(8,128)(2,1)}, u32[]{:S(2)}) copy-start(bf16[1,1,4,320,320]{4,3,2,1,0:T(8,128)(2,1)} %param.19) | copy-start | bytes 2457604
  0.0 17.0 %collective-permute-start.3 = (bf16[1,320,1024]{2,1,0:T(8,128)(2,1)}, bf16[1,320,1024]{2,1,0:T(8,128)(2,1)S(1)}, u32[]{:S(2)}, u32[]{:S(2)}) collective-permute-start(bf16[1,320,1024]{2,1,0:T(8,128)(2,1)} %bitcast.112), channel_id=1, source_target_pairs={{0,1},{1,2},{2,3},{4,5},{5,6},{6,7},{8,9},{9,10},{10,11},{12,13},{... | collective-permute-start | bytes 1966088 | tf_op jit(solution)/shard_map/ppermute | solution.py:14
  3.4 17.5 %collective-permute-start.4 = (bf16[1,320,1024]{2,1,0:T(8,128)(2,1)}, bf16[1,320,1024]{2,1,0:T(8,128)(2,1)}, u32[]{:S(2)}, u32[]{:S(2)}) collective-permute-start(bf16[1,320,1024]{2,1,0:T(8,128)(2,1)} %bitcast.113), channel_id=1, source_target_pairs={{1,0},{2,1},{3,2},{5,4},{6,5},{7,6},{9,8},{10,9},{11,10},{13,12},{... | collective-permute-start | bytes 1966088 | tf_op jit(solution)/shard_map/ppermute | solution.py:15
  4.7 23.0 %collective-permute-start.2 = (bf16[1,320,1024]{2,1,0:T(8,128)(2,1)}, bf16[1,320,1024]{2,1,0:T(8,128)(2,1)}, u32[]{:S(2)}, u32[]{:S(2)}) collective-permute-start(bf16[1,320,1024]{2,1,0:T(8,128)(2,1)} %bitcast.114), channel_id=1, source_target_pairs={{4,0},{8,4},{12,8},{16,12},{20,16},{24,20},{28,24},{5,1},{9,5},{13... | collective-permute-start | bytes 1966088 | tf_op jit(solution)/shard_map/ppermute | solution.py:23
  17.0 0.8 copy-start.4
  24.8 2.9 %copy-start.2 = (bf16[1,1,2,320,320]{4,3,2,1,0:T(8,128)(2,1)S(1)}, bf16[1,1,2,320,320]{4,3,2,1,0:T(8,128)(2,1)}, u32[]{:S(2)}) copy-start(bf16[1,1,2,320,320]{4,3,2,1,0:T(8,128)(2,1)} %param.18) | copy-start | bytes 1228804
  24.8 2.9 %copy-start.3 = (bf16[1,1,320,1024]{3,2,1,0:T(8,128)(2,1)S(1)}, bf16[1,1,320,1024]{3,2,1,0:T(8,128)(2,1)}, u32[]{:S(2)}) copy-start(bf16[1,1,320,1024]{3,2,1,0:T(8,128)(2,1)} %param.16) | copy-start | bytes 1966084
  29.3 2.8 %copy-start.1 = (bf16[1,1,320,320]{3,2,1,0:T(8,128)(2,1)S(1)}, bf16[1,1,320,320]{3,2,1,0:T(8,128)(2,1)}, u32[]{:S(2)}) copy-start(bf16[1,1,320,320]{3,2,1,0:T(8,128)(2,1)} %param.20) | copy-start | bytes 614404
  32.2 7.4 %collective-permute-start = (bf16[1,320,256]{2,1,0:T(8,128)(2,1)}, bf16[1,320,256]{2,1,0:T(8,128)(2,1)S(1)}, u32[]{:S(2)}, u32[]{:S(2)}) collective-permute-start(bf16[1,320,256]{2,1,0:T(8,128)(2,1)} %get-tuple-element.540), channel_id=1, source_target_pairs={{0,4},{4,8},{8,12},{12,16},{16,20},{20,24},{24,28},{1,5},{5,9},{9,... | collective-permute-start | bytes 491528 | tf_op jit(solution)/shard_map/while/body/eval_jaxpr/ppermute | solution.py:23
  40.2 7.7 %collective-permute-start = (bf16[1,320,256]{2,1,0:T(8,128)(2,1)}, bf16[1,320,256]{2,1,0:T(8,128)(2,1)S(1)}, u32[]{:S(2)}, u32[]{:S(2)}) collective-permute-start(bf16[1,320,256]{2,1,0:T(8,128)(2,1)} %get-tuple-element.540), channel_id=1, source_target_pairs={{0,4},{4,8},{8,12},{12,16},{16,20},{20,24},{24,28},{1,5},{5,9},{9,... | collective-permute-start | bytes 491528 | tf_op jit(solution)/shard_map/while/body/eval_jaxpr/ppermute | solution.py:23
  48.6 7.7 %collective-permute-start = (bf16[1,320,256]{2,1,0:T(8,128)(2,1)}, bf16[1,320,256]{2,1,0:T(8,128)(2,1)S(1)}, u32[]{:S(2)}, u32[]{:S(2)}) collective-permute-start(bf16[1,320,256]{2,1,0:T(8,128)(2,1)} %get-tuple-element.540), channel_id=1, source_target_pairs={{0,4},{4,8},{8,12},{12,16},{16,20},{20,24},{24,28},{1,5},{5,9},{9,... | collective-permute-start | bytes 491528 | tf_op jit(solution)/shard_map/while/body/eval_jaxpr/ppermute | solution.py:23
  57.0 7.7 %collective-permute-start = (bf16[1,320,256]{2,1,0:T(8,128)(2,1)}, bf16[1,320,256]{2,1,0:T(8,128)(2,1)S(1)}, u32[]{:S(2)}, u32[]{:S(2)}) collective-permute-start(bf16[1,320,256]{2,1,0:T(8,128)(2,1)} %get-tuple-element.540), channel_id=1, source_target_pairs={{0,4},{4,8},{8,12},{12,16},{16,20},{20,24},{24,28},{1,5},{5,9},{9,... | collective-permute-start | bytes 491528 | tf_op jit(solution)/shard_map/while/body/eval_jaxpr/ppermute | solution.py:23
  66.7 6.4 %collective-permute-start = (bf16[1,320,256]{2,1,0:T(8,128)(2,1)}, bf16[1,320,256]{2,1,0:T(8,128)(2,1)S(1)}, u32[]{:S(2)}, u32[]{:S(2)}) collective-permute-start(bf16[1,320,256]{2,1,0:T(8,128)(2,1)} %get-tuple-element.540), channel_id=1, source_target_pairs={{0,4},{4,8},{8,12},{12,16},{16,20},{20,24},{24,28},{1,5},{5,9},{9,... | collective-permute-start | bytes 491528 | tf_op jit(solution)/shard_map/while/body/eval_jaxpr/ppermute | solution.py:23
  75.2 7.7 %collective-permute-start = (bf16[1,320,256]{2,1,0:T(8,128)(2,1)}, bf16[1,320,256]{2,1,0:T(8,128)(2,1)S(1)}, u32[]{:S(2)}, u32[]{:S(2)}) collective-permute-start(bf16[1,320,256]{2,1,0:T(8,128)(2,1)} %get-tuple-element.540), channel_id=1, source_target_pairs={{0,4},{4,8},{8,12},{12,16},{16,20},{20,24},{24,28},{1,5},{5,9},{9,... | collective-permute-start | bytes 491528 | tf_op jit(solution)/shard_map/while/body/eval_jaxpr/ppermute | solution.py:23
  84.8 7.8 %collective-permute-start = (bf16[1,320,256]{2,1,0:T(8,128)(2,1)}, bf16[1,320,256]{2,1,0:T(8,128)(2,1)S(1)}, u32[]{:S(2)}, u32[]{:S(2)}) collective-permute-start(bf16[1,320,256]{2,1,0:T(8,128)(2,1)} %get-tuple-element.540), channel_id=1, source_target_pairs={{0,4},{4,8},{8,12},{12,16},{16,20},{20,24},{24,28},{1,5},{5,9},{9,... | collective-permute-start | bytes 491528 | tf_op jit(solution)/shard_map/while/body/eval_jaxpr/ppermute | solution.py:23
  94.6 7.7 %collective-permute-start = (bf16[1,320,256]{2,1,0:T(8,128)(2,1)}, bf16[1,320,256]{2,1,0:T(8,128)(2,1)S(1)}, u32[]{:S(2)}, u32[]{:S(2)}) collective-permute-start(bf16[1,320,256]{2,1,0:T(8,128)(2,1)} %get-tuple-element.540), channel_id=1, source_target_pairs={{0,4},{4,8},{8,12},{12,16},{16,20},{20,24},{24,28},{1,5},{5,9},{9,... | collective-permute-start | bytes 491528 | tf_op jit(solution)/shard_map/while/body/eval_jaxpr/ppermute | solution.py:23
  103.0 9.1 %collective-permute-start = (bf16[1,320,256]{2,1,0:T(8,128)(2,1)}, bf16[1,320,256]{2,1,0:T(8,128)(2,1)S(1)}, u32[]{:S(2)}, u32[]{:S(2)}) collective-permute-start(bf16[1,320,256]{2,1,0:T(8,128)(2,1)} %get-tuple-element.540), channel_id=1, source_target_pairs={{0,4},{4,8},{8,12},{12,16},{16,20},{20,24},{24,28},{1,5},{5,9},{9,... | collective-permute-start | bytes 491528 | tf_op jit(solution)/shard_map/while/body/eval_jaxpr/ppermute | solution.py:23
  112.7 7.7 %collective-permute-start = (bf16[1,320,256]{2,1,0:T(8,128)(2,1)}, bf16[1,320,256]{2,1,0:T(8,128)(2,1)S(1)}, u32[]{:S(2)}, u32[]{:S(2)}) collective-permute-start(bf16[1,320,256]{2,1,0:T(8,128)(2,1)} %get-tuple-element.540), channel_id=1, source_target_pairs={{0,4},{4,8},{8,12},{12,16},{16,20},{20,24},{24,28},{1,5},{5,9},{9,... | collective-permute-start | bytes 491528 | tf_op jit(solution)/shard_map/while/body/eval_jaxpr/ppermute | solution.py:23
  121.1 7.7 %collective-permute-start = (bf16[1,320,256]{2,1,0:T(8,128)(2,1)}, bf16[1,320,256]{2,1,0:T(8,128)(2,1)S(1)}, u32[]{:S(2)}, u32[]{:S(2)}) collective-permute-start(bf16[1,320,256]{2,1,0:T(8,128)(2,1)} %get-tuple-element.540), channel_id=1, source_target_pairs={{0,4},{4,8},{8,12},{12,16},{16,20},{20,24},{24,28},{1,5},{5,9},{9,... | collective-permute-start | bytes 491528 | tf_op jit(solution)/shard_map/while/body/eval_jaxpr/ppermute | solution.py:23
  129.5 14.4 %collective-permute-start.5 = (bf16[1,320,1024]{2,1,0:T(8,128)(2,1)}, bf16[1,320,1024]{2,1,0:T(8,128)(2,1)S(1)}, u32[]{:S(2)}, u32[]{:S(2)}) collective-permute-start(bf16[1,320,1024]{2,1,0:T(8,128)(2,1)} %get-tuple-element.374), channel_id=1, source_target_pairs={{0,1},{1,2},{2,3},{4,5},{5,6},{6,7},{8,9},{9,10},{10,11},{12,13},{... | collective-permute-start | bytes 1966088 | tf_op jit(solution)/shard_map/ppermute | solution.py:14
  132.7 15.3 %collective-permute-start.6 = (bf16[1,320,1024]{2,1,0:T(8,128)(2,1)}, bf16[1,320,1024]{2,1,0:T(8,128)(2,1)}, u32[]{:S(2)}, u32[]{:S(2)}) collective-permute-start(bf16[1,320,1024]{2,1,0:T(8,128)(2,1)} %get-tuple-element.374), channel_id=1, source_target_pairs={{1,0},{2,1},{3,2},{5,4},{6,5},{7,6},{9,8},{10,9},{11,10},{13,12},{... | collective-permute-start | bytes 1966088 | tf_op jit(solution)/shard_map/ppermute | solution.py:15
  143.9 0.9 copy-start.5
  156.9 7.7 %collective-permute-start.1 = (bf16[1,320,256]{2,1,0:T(8,128)(2,1)}, bf16[1,320,256]{2,1,0:T(8,128)(2,1)S(1)}, u32[]{:S(2)}, u32[]{:S(2)}) collective-permute-start(bf16[1,320,256]{2,1,0:T(8,128)(2,1)} %get-tuple-element.571), channel_id=1, source_target_pairs={{4,0},{8,4},{12,8},{16,12},{20,16},{24,20},{28,24},{5,1},{9,5},{13... | collective-permute-start | bytes 491528 | tf_op jit(solution)/shard_map/while/body/eval_jaxpr/ppermute | solution.py:23
  165.3 7.7 %collective-permute-start.1 = (bf16[1,320,256]{2,1,0:T(8,128)(2,1)}, bf16[1,320,256]{2,1,0:T(8,128)(2,1)S(1)}, u32[]{:S(2)}, u32[]{:S(2)}) collective-permute-start(bf16[1,320,256]{2,1,0:T(8,128)(2,1)} %get-tuple-element.571), channel_id=1, source_target_pairs={{4,0},{8,4},{12,8},{16,12},{20,16},{24,20},{28,24},{5,1},{9,5},{13... | collective-permute-start | bytes 491528 | tf_op jit(solution)/shard_map/while/body/eval_jaxpr/ppermute | solution.py:23
  173.7 7.7 %collective-permute-start.1 = (bf16[1,320,256]{2,1,0:T(8,128)(2,1)}, bf16[1,320,256]{2,1,0:T(8,128)(2,1)S(1)}, u32[]{:S(2)}, u32[]{:S(2)}) collective-permute-start(bf16[1,320,256]{2,1,0:T(8,128)(2,1)} %get-tuple-element.571), channel_id=1, source_target_pairs={{4,0},{8,4},{12,8},{16,12},{20,16},{24,20},{28,24},{5,1},{9,5},{13... | collective-permute-start | bytes 491528 | tf_op jit(solution)/shard_map/while/body/eval_jaxpr/ppermute | solution.py:23
  182.1 7.7 %collective-permute-start.1 = (bf16[1,320,256]{2,1,0:T(8,128)(2,1)}, bf16[1,320,256]{2,1,0:T(8,128)(2,1)S(1)}, u32[]{:S(2)}, u32[]{:S(2)}) collective-permute-start(bf16[1,320,256]{2,1,0:T(8,128)(2,1)} %get-tuple-element.571), channel_id=1, source_target_pairs={{4,0},{8,4},{12,8},{16,12},{20,16},{24,20},{28,24},{5,1},{9,5},{13... | collective-permute-start | bytes 491528 | tf_op jit(solution)/shard_map/while/body/eval_jaxpr/ppermute | solution.py:23
  190.5 7.7 %collective-permute-start.1 = (bf16[1,320,256]{2,1,0:T(8,128)(2,1)}, bf16[1,320,256]{2,1,0:T(8,128)(2,1)S(1)}, u32[]{:S(2)}, u32[]{:S(2)}) collective-permute-start(bf16[1,320,256]{2,1,0:T(8,128)(2,1)} %get-tuple-element.571), channel_id=1, source_target_pairs={{4,0},{8,4},{12,8},{16,12},{20,16},{24,20},{28,24},{5,1},{9,5},{13... | collective-permute-start | bytes 491528 | tf_op jit(solution)/shard_map/while/body/eval_jaxpr/ppermute | solution.py:23
  199.5 7.7 %collective-permute-start.1 = (bf16[1,320,256]{2,1,0:T(8,128)(2,1)}, bf16[1,320,256]{2,1,0:T(8,128)(2,1)S(1)}, u32[]{:S(2)}, u32[]{:S(2)}) collective-permute-start(bf16[1,320,256]{2,1,0:T(8,128)(2,1)} %get-tuple-element.571), channel_id=1, source_target_pairs={{4,0},{8,4},{12,8},{16,12},{20,16},{24,20},{28,24},{5,1},{9,5},{13... | collective-permute-start | bytes 491528 | tf_op jit(solution)/shard_map/while/body/eval_jaxpr/ppermute | solution.py:23
  208.6 7.7 %collective-permute-start.1 = (bf16[1,320,256]{2,1,0:T(8,128)(2,1)}, bf16[1,320,256]{2,1,0:T(8,128)(2,1)S(1)}, u32[]{:S(2)}, u32[]{:S(2)}) collective-permute-start(bf16[1,320,256]{2,1,0:T(8,128)(2,1)} %get-tuple-element.571), channel_id=1, source_target_pairs={{4,0},{8,4},{12,8},{16,12},{20,16},{24,20},{28,24},{5,1},{9,5},{13... | collective-permute-start | bytes 491528 | tf_op jit(solution)/shard_map/while/body/eval_jaxpr/ppermute | solution.py:23
  217.6 7.7 %collective-permute-start.1 = (bf16[1,320,256]{2,1,0:T(8,128)(2,1)}, bf16[1,320,256]{2,1,0:T(8,128)(2,1)S(1)}, u32[]{:S(2)}, u32[]{:S(2)}) collective-permute-start(bf16[1,320,256]{2,1,0:T(8,128)(2,1)} %get-tuple-element.571), channel_id=1, source_target_pairs={{4,0},{8,4},{12,8},{16,12},{20,16},{24,20},{28,24},{5,1},{9,5},{13... | collective-permute-start | bytes 491528 | tf_op jit(solution)/shard_map/while/body/eval_jaxpr/ppermute | solution.py:23
  226.6 7.7 %collective-permute-start.1 = (bf16[1,320,256]{2,1,0:T(8,128)(2,1)}, bf16[1,320,256]{2,1,0:T(8,128)(2,1)S(1)}, u32[]{:S(2)}, u32[]{:S(2)}) collective-permute-start(bf16[1,320,256]{2,1,0:T(8,128)(2,1)} %get-tuple-element.571), channel_id=1, source_target_pairs={{4,0},{8,4},{12,8},{16,12},{20,16},{24,20},{28,24},{5,1},{9,5},{13... | collective-permute-start | bytes 491528 | tf_op jit(solution)/shard_map/while/body/eval_jaxpr/ppermute | solution.py:23
  235.0 7.7 %collective-permute-start.1 = (bf16[1,320,256]{2,1,0:T(8,128)(2,1)}, bf16[1,320,256]{2,1,0:T(8,128)(2,1)S(1)}, u32[]{:S(2)}, u32[]{:S(2)}) collective-permute-start(bf16[1,320,256]{2,1,0:T(8,128)(2,1)} %get-tuple-element.571), channel_id=1, source_target_pairs={{4,0},{8,4},{12,8},{16,12},{20,16},{24,20},{28,24},{5,1},{9,5},{13... | collective-permute-start | bytes 491528 | tf_op jit(solution)/shard_map/while/body/eval_jaxpr/ppermute | solution.py:23
  243.5 7.7 %collective-permute-start.1 = (bf16[1,320,256]{2,1,0:T(8,128)(2,1)}, bf16[1,320,256]{2,1,0:T(8,128)(2,1)S(1)}, u32[]{:S(2)}, u32[]{:S(2)}) collective-permute-start(bf16[1,320,256]{2,1,0:T(8,128)(2,1)} %get-tuple-element.571), channel_id=1, source_target_pairs={{4,0},{8,4},{12,8},{16,12},{20,16},{24,20},{28,24},{5,1},{9,5},{13... | collective-permute-start | bytes 491528 | tf_op jit(solution)/shard_map/while/body/eval_jaxpr/ppermute | solution.py:23
where the time goes:
time: 253 us; the launch traced here: 252 us
  waiting for transfers between devices  115 us (45%)
  starting transfers between devices  89.5 us (35%)
  matrix products  21 us (8%)
  local copies, waits for them, and re-layouts  20.9 us (8%)
  other arithmetic  4.72 us (2%)
    ppermute x23, waiting for transfers between devices, from_behind(): lax.ppermute(value, axis, [(source, source + steps) for source in range(f...  91.9 us
    ppermute x23, starting transfers between devices, from_behind(): lax.ppermute(value, axis, [(source, source + steps) for source in range(f...  80.4 us
    ppermute x2, waiting for transfers between devices, with_halo(): before = lax.ppermute(last, axis, up)  16.9 us
    dot_general x13, matrix products, apply_block(): jnp.einsum('eij,ejr->eir', blocks, states, preferred_element_type=jnp.flo...  14.7 us
    another operation x18, local copies, waits for them, and re-layouts  12.5 us
    ppermute x2, starting transfers between devices, with_halo(): before = lax.ppermute(last, axis, up)  6.55 us
    ppermute x2, waiting for transfers between devices, with_halo(): after = lax.ppermute(first, axis, down)  6.29 us
    dot_general x2, matrix products, gather_faces(): jnp.einsum('efij,efjr->eir', face_blocks, picked, preferred_element_type=...  6.27 us
  transfers between devices with their start and end apart: 27, of which 26 were waited for; matrix products, arithmetic and copies ran while one was open for 4% of the time, Pallas kernels for 0%

commit v1 on v0

v1 whole, which is shorter than its diff:
```python
import functools

import jax
import jax.numpy as jnp
from jax import lax
from jax.experimental import pallas as pl
from jax.experimental.pallas import tpu as pltpu
from jax.sharding import PartitionSpec as P

PANELS = 4
LAG_FORWARD = (1, 1)
LAG_HALO = 1
LAG_BACKWARD = (1, 2)


def dot(a, b):
    return jnp.dot(a, b, preferred_element_type=jnp.float32)


def kernel(
    planes, strips, panels,
    right_hbm, old_hbm, plane_hbm, face_hbm, inverse_hbm, links,
    out_hbm,
    right, plane, face, inverse,
    old_stack, half_stack, old_weights, half_weights,
    lower_step, upper_step, own_step, pair_step, chip_step,
    base, rest, share, pair_share, half_in, final_in, final_out,
    load_sem, own_sem, store_sem,
    old_send, old_recv, halo_send, halo_recv,
    step_send, step_recv, share_send, share_recv,
    chain_send, relay_send, half_recv, final_recv,
):
    p, g = lax.axis_index("gx"), lax.axis_index("gy")
    size = inverse.shape[0]
    width = final_out.shape[2]
    odd = lax.rem(p, 2)
    even = odd == 0
    partner = p + 1 - 2 * odd
    chip, chips = p // 2, planes // 2
    has_prev, has_next = p >= 2, p < planes - 2
    below, above = g > 0, g < strips - 1

    def remote(src, dst, send, recv, plane_to, strip_to):
        return pltpu.make_async_remote_copy(
            src_ref=src, dst_ref=dst, send_sem=send, recv_sem=recv,
            device_id=(plane_to, strip_to), device_id_type=pl.DeviceIdType.MESH,
        )

    def columns(k):
        return pl.ds(pl.multiple_of(k * width, width), width)

    def rows(n):
        return pl.ds(n * size, size)

    def each(body):
        lax.fori_loop(0, panels, lambda k, c: (body(k), c)[1], 0)

    def old_panel(k):
        return old_hbm.at[0, 0, :, columns(k)]

    def old_up(k):
        return remote(old_panel(k), old_stack.at[k, rows(1)], old_send.at[k, 0], old_recv.at[k, 0], p, g + 1)

    def old_down(k):
        return remote(old_panel(k), old_stack.at[k, rows(3)], old_send.at[k, 1], old_recv.at[k, 1], p, g - 1)

    def old_back(k):
        return remote(old_panel(k), old_stack.at[k, rows(0)], old_send.at[k, 2], old_recv.at[k, 2], p - 1, g)

    def old_own(k):
        return pltpu.make_async_copy(old_panel(k), old_stack.at[k, rows(2)], own_sem.at[k])

    def halo_up(k):
        return remote(half_stack.at[k, rows(1)], half_stack.at[k, rows(0)], halo_send.at[k, 0], halo_recv.at[k, 0], p, g + 1)

    def halo_down(k):
        return remote(half_stack.at[k, rows(1)], half_stack.at[k, rows(2)], halo_send.at[k, 1], halo_recv.at[k, 1], p, g - 1)

    def step_copy():
        return remote(own_step, pair_step, step_send, step_recv, partner, g)

    def share_copy(k):
        return remote(share.at[k], pair_share.at[k], share_send.at[k], share_recv.at[k], partner, g)

    def half_chain(k):
        return remote(half_stack.at[k, rows(1)], half_in.at[k], chain_send.at[k], half_recv.at[k], p + 2, g)

    def half_relay(k):
        return remote(half_in.at[k], half_in.at[k], relay_send.at[k], half_recv.at[k], partner, g)

    def final_chain(k):
        return remote(final_out.at[k], final_in.at[k], chain_send.at[k], final_recv.at[k], p - 2, g)

    def final_relay(k):
        return remote(final_in.at[k], final_in.at[k], relay_send.at[k], final_recv.at[k], partner, g)

    def store(k):
        return pltpu.make_async_copy(final_out.at[k], out_hbm.at[0, 0, :, columns(k)], store_sem.at[k])

    loads = [
        pltpu.make_async_copy(plane_hbm.at[0, 0], plane, load_sem.at[0]),
        pltpu.make_async_copy(inverse_hbm.at[0, 0], inverse, load_sem.at[1]),
        pltpu.make_async_copy(face_hbm.at[0, 0], face, load_sem.at[2]),
        pltpu.make_async_copy(right_hbm.at[0, 0], right, load_sem.at[3]),
    ]

    barrier = pltpu.get_barrier_semaphore()
    greeted = (
        (below, p, g - 1), (above, p, g + 1), (p > 0, p - 1, g), (p < planes - 1, p + 1, g),
        (has_prev, p - 2, g), (has_next, p + 2, g),
    )
    for there, plane_to, strip_to in greeted:
        @pl.when(there)
        def _():
            pl.semaphore_signal(barrier, inc=1, device_id=(plane_to, strip_to), device_id_type=pl.DeviceIdType.MESH)
    for copy in loads:
        copy.start()
    each(lambda k: old_own(k).start())
    pl.semaphore_wait(barrier, sum(there.astype(jnp.int32) for there, _, _ in greeted))

    def send_old(k):
        pl.when(above)(lambda: old_up(k).start())
        pl.when(below)(lambda: old_down(k).start())
        pl.when(p > 0)(lambda: old_back(k).start())

    each(send_old)

    nothing = jnp.zeros((panels, size, width), jnp.bfloat16)

    @pl.when(jnp.logical_not(below))
    def _():
        old_stack[:, rows(1)] = nothing
        half_stack[:, rows(0)] = nothing

    @pl.when(jnp.logical_not(above))
    def _():
        old_stack[:, rows(3)] = nothing
        half_stack[:, rows(2)] = nothing

    @pl.when(p == planes - 1)
    def _():
        old_stack[:, rows(0)] = nothing

    @pl.when(jnp.logical_not(has_prev))
    def _():
        half_in[...] = nothing

    @pl.when(jnp.logical_not(has_next))
    def _():
        final_in[...] = nothing

    loads[0].wait()
    loads[1].wait()
    lower_step[...] = dot(inverse[...], plane[0]).astype(jnp.bfloat16)
    upper_step[...] = dot(inverse[...], plane[1]).astype(jnp.bfloat16)

    @pl.when(even)
    def _():
        own_step[...] = lower_step[...]

    @pl.when(odd == 1)
    def _():
        own_step[...] = upper_step[...]

    step_copy().start()
    loads[2].wait()
    old_weights[:, 0:size] = plane[1]
    for candidate in range(3):
        total = face[0 if candidate == 0 else 1].astype(jnp.float32) if candidate != 1 else None
        for f in (2, 3):
            named = jnp.where(links[0, 0, f] == candidate, 1.0, 0.0)
            term = face[f].astype(jnp.float32) * named
            total = term if total is None else total + term
        total = total.astype(jnp.bfloat16)
        old_weights[:, (candidate + 1) * size : (candidate + 2) * size] = total
        half_weights[:, candidate * size : (candidate + 1) * size] = total
    loads[3].wait()
    step_copy().wait()

    @pl.when(even)
    def _():
        chip_step[...] = dot(upper_step[...], pair_step[...]).astype(jnp.bfloat16)

    @pl.when(odd == 1)
    def _():
        chip_step[...] = dot(lower_step[...], pair_step[...]).astype(jnp.bfloat16)

    def prepare(k):
        old_own(k).wait()
        pl.when(p < planes - 1)(lambda: old_back(k).wait_recv())
        pl.when(below)(lambda: old_up(k).wait_recv())
        pl.when(above)(lambda: old_down(k).wait_recv())
        old_sum = right[:, columns(k)].astype(jnp.float32) - dot(old_weights[...], old_stack[k])
        value = dot(inverse[...], old_sum.astype(jnp.bfloat16))
        base[k] = value

        @pl.when(even)
        def _():
            share[k] = value.astype(jnp.bfloat16)
            share_copy(k).start()

    def send_half(k):
        pl.when(above)(lambda: halo_up(k).start())
        pl.when(below)(lambda: halo_down(k).start())

    def forward(k):
        @pl.when(odd == 1)
        def _():
            share_copy(k).wait_recv()
            before = pair_share[k]
            value = base[k] - dot(lower_step[...], before)

            @pl.when(has_prev)
            def _():
                half_chain(k).wait_recv()
                half_relay(k).start()

            arrived = half_in[k]
            half_stack[k, rows(1)] = (value + dot(chip_step[...], arrived)).astype(jnp.bfloat16)
            pl.when(has_next)(lambda: half_chain(k).start())
            send_half(k)
            prior = (before.astype(jnp.float32) - dot(pair_step[...], arrived)).astype(jnp.bfloat16)
            rest[k] = right[:, columns(k)].astype(jnp.float32) - dot(plane[0], prior)

        @pl.when(even)
        def _():
            pl.when(has_prev)(lambda: half_relay(k).wait_recv())
            arrived = half_in[k]
            half_stack[k, rows(1)] = (base[k] - dot(lower_step[...], arrived)).astype(jnp.bfloat16)
            send_half(k)
            rest[k] = right[:, columns(k)].astype(jnp.float32) - dot(plane[0], arrived)

    def turn_round(k):
        pl.when(below)(lambda: halo_up(k).wait_recv())
        pl.when(above)(lambda: halo_down(k).wait_recv())
        half_sum = rest[k] - dot(half_weights[...], half_stack[k])
        value = dot(inverse[...], half_sum.astype(jnp.bfloat16))
        base[k] = value

        @pl.when(odd == 1)
        def _():
            share[k] = value.astype(jnp.bfloat16)
            share_copy(k).start()

    def backward(k):
        @pl.when(even)
        def _():
            share_copy(k).wait_recv()
            value = base[k] - dot(upper_step[...], pair_share[k])

            @pl.when(has_next)
            def _():
                final_chain(k).wait_recv()
                final_relay(k).start()

            final_out[k] = (value + dot(chip_step[...], final_in[k])).astype(jnp.bfloat16)
            pl.when(has_prev)(lambda: final_chain(k).start())

        @pl.when(odd == 1)
        def _():
            pl.when(has_next)(lambda: final_relay(k).wait_recv())
            final_out[k] = (base[k] - dot(upper_step[...], final_in[k])).astype(jnp.bfloat16)

        store(k).start()

    to_forward = jnp.minimum(panels, LAG_FORWARD[0] + LAG_FORWARD[1] * chip)
    to_turn = to_forward + LAG_HALO
    to_backward = to_turn + jnp.minimum(panels, LAG_BACKWARD[0] + LAG_BACKWARD[1] * (chips - 1 - chip))

    def turn(t, carry):
        pl.when(t < panels)(lambda: prepare(t))
        for lag, stage in ((to_forward, forward), (to_turn, turn_round), (to_backward, backward)):
            k = t - lag
            pl.when((k >= 0) & (k < panels))(functools.partial(stage, k))
        return carry

    lax.fori_loop(0, panels + to_backward, turn, 0)

    def finish(k):
        store(k).wait()
        share_copy(k).wait_send()

        @pl.when(above)
        def _():
            old_up(k).wait_send()
            halo_up(k).wait_send()

        @pl.when(below)
        def _():
            old_down(k).wait_send()
            halo_down(k).wait_send()

        pl.when(p > 0)(lambda: old_back(k).wait_send())

        @pl.when(odd == 1)
        def _():
            pl.when(has_next)(lambda: half_chain(k).wait_send())
            pl.when(has_prev)(lambda: half_relay(k).wait_send())

        @pl.when(even)
        def _():
            pl.when(has_prev)(lambda: final_chain(k).wait_send())
            pl.when(has_next)(lambda: final_relay(k).wait_send())

    each(finish)


def local(planes, strips, right_sides, old_state, plane_coupling, face_coupling, diag_inverse, neighbours):
    size, total = right_sides.shape[2:]
    n = PANELS
    width = total // n
    half = functools.partial(pltpu.VMEM, dtype=jnp.bfloat16)
    single = functools.partial(pltpu.VMEM, dtype=jnp.float32)
    dma = pltpu.SemaphoreType.DMA
    anywhere = pl.BlockSpec(memory_space=pl.ANY)
    return pl.pallas_call(
        functools.partial(kernel, planes, strips, n),
        out_shape=jax.ShapeDtypeStruct(right_sides.shape, jnp.bfloat16),
        in_specs=[anywhere] * 5 + [pl.BlockSpec(memory_space=pltpu.SMEM)],
        out_specs=anywhere,
        scratch_shapes=[
            half((size, total)), half((2, size, size)), half((4, size, size)), half((size, size)),
            half((n, 4 * size, width)), half((n, 3 * size, width)), half((size, 4 * size)), half((size, 3 * size)),
            half((size, size)), half((size, size)), half((size, size)), half((size, size)), half((size, size)),
            single((n, size, width)), single((n, size, width)), half((n, size, width)), half((n, size, width)),
            half((n, size, width)), half((n, size, width)), half((n, size, width)),
            dma((4,)), dma((n,)), dma((n,)),
            dma((n, 3)), dma((n, 3)), dma((n, 2)), dma((n, 2)),
            dma, dma, dma((n,)), dma((n,)),
            dma((n,)), dma((n,)), dma((n,)), dma((n,)),
        ],
        compiler_params=pltpu.CompilerParams(
            collective_id=0, has_side_effects=True, vmem_limit_bytes=48 * 2**20
        ),
    )(right_sides, old_state, plane_coupling, face_coupling, diag_inverse, neighbours)


def solution(mesh):
    specs = [P("gx", "gy", *[None] * n) for n in (2, 2, 3, 3, 2, 1)]
    run = functools.partial(local, mesh.shape["gx"], mesh.shape["gy"])
    return jax.shard_map(run, mesh=mesh, in_specs=tuple(specs), out_specs=specs[0], check_vma=False)
```

time: 253 us -> 72.6 us (0.29)
  the two profiles are of different devices: /device:TPU:3 before, /device:TPU:1 now
where the time goes in v1:
time: 72.6 us; the launch traced here: 72.3 us
  Pallas kernels  65.4 us (90%)
  local copies, waits for them, and re-layouts  6.84 us (9%)
    pallas_call x1, Pallas kernels, local(): pl.pallas_call(functools.partial(kernel, planes, strips, n), out_shape=ja...  65.4 us
    unnamed x13, local copies, waits for them, and re-layouts  6.84 us

profile of v1, /device:TPU:1, one launch (start us, length us, event | category | flops | bytes accessed | tf_op | source)
XLA Modules:
  0.0 72.3 jit_solution(495897662179981443)
XLA Ops:
  0.0 0.0 copy-start
  0.0 1.2 %copy-done = bf16[1,1,4,320,320]{4,3,2,1,0:T(8,128)(2,1)S(1)} copy-done((bf16[1,1,4,320,320]{4,3,2,1,0:T(8,128)(2,1)S(1)}, bf16[1,1,4,320,320]{4,3,2,1,0:T(8,128)(2,1)}, u32[]{:S(2)}) %copy-start) | copy-done | bytes 819224
  1.2 0.0 copy-start.1
  1.2 1.1 %copy-done.1 = bf16[1,1,320,1024]{3,2,1,0:T(8,128)(2,1)S(1)} copy-done((bf16[1,1,320,1024]{3,2,1,0:T(8,128)(2,1)S(1)}, bf16[1,1,320,1024]{3,2,1,0:T(8,128)(2,1)}, u32[]{:S(2)}) %copy-start.1) | copy-done | bytes 655384
  2.3 0.0 copy-start.2
  2.3 1.1 %copy-done.2 = bf16[1,1,320,1024]{3,2,1,0:T(8,128)(2,1)S(1)} copy-done((bf16[1,1,320,1024]{3,2,1,0:T(8,128)(2,1)S(1)}, bf16[1,1,320,1024]{3,2,1,0:T(8,128)(2,1)}, u32[]{:S(2)}) %copy-start.2) | copy-done | bytes 655384
  3.4 0.0 copy-start.3
  3.4 1.0 %copy-done.3 = bf16[1,1,2,320,320]{4,3,2,1,0:T(8,128)(2,1)S(1)} copy-done((bf16[1,1,2,320,320]{4,3,2,1,0:T(8,128)(2,1)S(1)}, bf16[1,1,2,320,320]{4,3,2,1,0:T(8,128)(2,1)}, u32[]{:S(2)}) %copy-start.3) | copy-done | bytes 409624
  4.4 0.0 copy-start.4
  4.4 0.9 %copy-done.4 = bf16[1,1,320,320]{3,2,1,0:T(8,128)(2,1)S(1)} copy-done((bf16[1,1,320,320]{3,2,1,0:T(8,128)(2,1)S(1)}, bf16[1,1,320,320]{3,2,1,0:T(8,128)(2,1)}, u32[]{:S(2)}) %copy-start.4) | copy-done | bytes 204824
  5.4 0.0 copy-start.5
  5.4 0.7 copy-done.5
  6.0 65.4 %shard_map.64 = bf16[1,1,320,1024]{3,2,1,0:T(8,128)(2,1)S(1)} custom-call(bf16[1,1,320,1024]{3,2,1,0:T(8,128)(2,1)S(1)} %copy-done.1, bf16[1,1,320,1024]{3,2,1,0:T(8,128)(2,1)S(1)} %copy-done.2, bf16[1,1,2,320,320]{4,3,2,1,0:T(8,128)(2,1)S(1)} %copy-done.3, bf16[1,1,4,320,320]{4,3,2,1,0:T(8,128)(2,1)S(1)} %copy-done, bf16[1,1,320,320]{3,2,1,0:T(8,128)(2,1)S(1)} %copy-done.4, ...), custom_call_target="tpu_custom_call" | custom-call | tf_op jit(solution)/shard_map/pallas_call | solution.py:316
  71.4 0.8 %copy.8 = bf16[1,1,320,1024]{3,2,1,0:T(8,128)(2,1)} copy(bf16[1,1,320,1024]{3,2,1,0:T(8,128)(2,1)S(1)} %shard_map.64) | data formatting | bytes 1310720
Async XLA Ops:
  0.0 1.2 %copy-start = (bf16[1,1,4,320,320]{4,3,2,1,0:T(8,128)(2,1)S(1)}, bf16[1,1,4,320,320]{4,3,2,1,0:T(8,128)(2,1)}, u32[]{:S(2)}) copy-start(bf16[1,1,4,320,320]{4,3,2,1,0:T(8,128)(2,1)} %face_hbm.1) | copy-start | bytes 2457604
  1.2 1.1 %copy-start.1 = (bf16[1,1,320,1024]{3,2,1,0:T(8,128)(2,1)S(1)}, bf16[1,1,320,1024]{3,2,1,0:T(8,128)(2,1)}, u32[]{:S(2)}) copy-start(bf16[1,1,320,1024]{3,2,1,0:T(8,128)(2,1)} %right_hbm.1) | copy-start | bytes 1966084
  2.3 1.1 %copy-start.2 = (bf16[1,1,320,1024]{3,2,1,0:T(8,128)(2,1)S(1)}, bf16[1,1,320,1024]{3,2,1,0:T(8,128)(2,1)}, u32[]{:S(2)}) copy-start(bf16[1,1,320,1024]{3,2,1,0:T(8,128)(2,1)} %old_hbm.1) | copy-start | bytes 1966084
  3.4 1.0 %copy-start.3 = (bf16[1,1,2,320,320]{4,3,2,1,0:T(8,128)(2,1)S(1)}, bf16[1,1,2,320,320]{4,3,2,1,0:T(8,128)(2,1)}, u32[]{:S(2)}) copy-start(bf16[1,1,2,320,320]{4,3,2,1,0:T(8,128)(2,1)} %plane_hbm.1) | copy-start | bytes 1228804
  4.4 0.9 %copy-start.4 = (bf16[1,1,320,320]{3,2,1,0:T(8,128)(2,1)S(1)}, bf16[1,1,320,320]{3,2,1,0:T(8,128)(2,1)}, u32[]{:S(2)}) copy-start(bf16[1,1,320,320]{3,2,1,0:T(8,128)(2,1)} %inverse_hbm.1) | copy-start | bytes 614404
  5.4 0.7 copy-start.5

commit v2 on v1

--- a/solution.py
+++ b/solution.py
@@ -7,10 +7,10 @@
 from jax.experimental.pallas import tpu as pltpu
 from jax.sharding import PartitionSpec as P
 
-PANELS = 4
-LAG_FORWARD = (1, 1)
-LAG_HALO = 1
-LAG_BACKWARD = (1, 2)
+PANELS = 8
+LAG_FORWARD = (2, 2)
+LAG_HALO = 3
+LAG_BACKWARD = (3, 6)
 
 
 def dot(a, b):

time: 72.6 us -> 67.8 us (0.934)
  Pallas kernels: 65.4 us -> 60.6 us
    pallas_call x1, Pallas kernels: 65.4 us -> 60.6 us  [local(): pl.pallas_call(functools.partial(kernel, planes, strips, n), out_shape=ja...]
where the time goes in v2:
time: 67.8 us; the launch traced here: 67.5 us
  Pallas kernels  60.6 us (89%)
  local copies, waits for them, and re-layouts  6.84 us (10%)
    pallas_call x1, Pallas kernels, local(): pl.pallas_call(functools.partial(kernel, planes, strips, n), out_shape=ja...  60.6 us
    unnamed x13, local copies, waits for them, and re-layouts  6.84 us

profile of v2, /device:TPU:1, one launch (start us, length us, event | category | flops | bytes accessed | tf_op | source)
XLA Modules:
  0.0 67.5 jit_solution(5284449502361561965)
XLA Ops:
  0.0 0.0 copy-start
  0.0 1.2 %copy-done = bf16[1,1,4,320,320]{4,3,2,1,0:T(8,128)(2,1)S(1)} copy-done((bf16[1,1,4,320,320]{4,3,2,1,0:T(8,128)(2,1)S(1)}, bf16[1,1,4,320,320]{4,3,2,1,0:T(8,128)(2,1)}, u32[]{:S(2)}) %copy-start) | copy-done | bytes 819224
  1.2 0.0 copy-start.1
  1.2 1.1 %copy-done.1 = bf16[1,1,320,1024]{3,2,1,0:T(8,128)(2,1)S(1)} copy-done((bf16[1,1,320,1024]{3,2,1,0:T(8,128)(2,1)S(1)}, bf16[1,1,320,1024]{3,2,1,0:T(8,128)(2,1)}, u32[]{:S(2)}) %copy-start.1) | copy-done | bytes 655384
  2.3 0.0 copy-start.2
  2.3 1.1 %copy-done.2 = bf16[1,1,320,1024]{3,2,1,0:T(8,128)(2,1)S(1)} copy-done((bf16[1,1,320,1024]{3,2,1,0:T(8,128)(2,1)S(1)}, bf16[1,1,320,1024]{3,2,1,0:T(8,128)(2,1)}, u32[]{:S(2)}) %copy-start.2) | copy-done | bytes 655384
  3.4 0.0 copy-start.3
  3.4 1.0 %copy-done.3 = bf16[1,1,2,320,320]{4,3,2,1,0:T(8,128)(2,1)S(1)} copy-done((bf16[1,1,2,320,320]{4,3,2,1,0:T(8,128)(2,1)S(1)}, bf16[1,1,2,320,320]{4,3,2,1,0:T(8,128)(2,1)}, u32[]{:S(2)}) %copy-start.3) | copy-done | bytes 409624
  4.4 0.0 copy-start.4
  4.4 0.9 %copy-done.4 = bf16[1,1,320,320]{3,2,1,0:T(8,128)(2,1)S(1)} copy-done((bf16[1,1,320,320]{3,2,1,0:T(8,128)(2,1)S(1)}, bf16[1,1,320,320]{3,2,1,0:T(8,128)(2,1)}, u32[]{:S(2)}) %copy-start.4) | copy-done | bytes 204824
  5.4 0.0 copy-start.5
  5.4 0.7 copy-done.5
  6.0 60.6 %shard_map.64 = bf16[1,1,320,1024]{3,2,1,0:T(8,128)(2,1)S(1)} custom-call(bf16[1,1,320,1024]{3,2,1,0:T(8,128)(2,1)S(1)} %copy-done.1, bf16[1,1,320,1024]{3,2,1,0:T(8,128)(2,1)S(1)} %copy-done.2, bf16[1,1,2,320,320]{4,3,2,1,0:T(8,128)(2,1)S(1)} %copy-done.3, bf16[1,1,4,320,320]{4,3,2,1,0:T(8,128)(2,1)S(1)} %copy-done, bf16[1,1,320,320]{3,2,1,0:T(8,128)(2,1)S(1)} %copy-done.4, ...), custom_call_target="tpu_custom_call" | custom-call | tf_op jit(solution)/shard_map/pallas_call | solution.py:316
  66.6 0.8 %copy.8 = bf16[1,1,320,1024]{3,2,1,0:T(8,128)(2,1)} copy(bf16[1,1,320,1024]{3,2,1,0:T(8,128)(2,1)S(1)} %shard_map.64) | data formatting | bytes 1310720
Async XLA Ops:
  0.0 1.2 %copy-start = (bf16[1,1,4,320,320]{4,3,2,1,0:T(8,128)(2,1)S(1)}, bf16[1,1,4,320,320]{4,3,2,1,0:T(8,128)(2,1)}, u32[]{:S(2)}) copy-start(bf16[1,1,4,320,320]{4,3,2,1,0:T(8,128)(2,1)} %face_hbm.1) | copy-start | bytes 2457604
  1.2 1.1 %copy-start.1 = (bf16[1,1,320,1024]{3,2,1,0:T(8,128)(2,1)S(1)}, bf16[1,1,320,1024]{3,2,1,0:T(8,128)(2,1)}, u32[]{:S(2)}) copy-start(bf16[1,1,320,1024]{3,2,1,0:T(8,128)(2,1)} %right_hbm.1) | copy-start | bytes 1966084
  2.3 1.1 %copy-start.2 = (bf16[1,1,320,1024]{3,2,1,0:T(8,128)(2,1)S(1)}, bf16[1,1,320,1024]{3,2,1,0:T(8,128)(2,1)}, u32[]{:S(2)}) copy-start(bf16[1,1,320,1024]{3,2,1,0:T(8,128)(2,1)} %old_hbm.1) | copy-start | bytes 1966084
  3.4 1.0 %copy-start.3 = (bf16[1,1,2,320,320]{4,3,2,1,0:T(8,128)(2,1)S(1)}, bf16[1,1,2,320,320]{4,3,2,1,0:T(8,128)(2,1)}, u32[]{:S(2)}) copy-start(bf16[1,1,2,320,320]{4,3,2,1,0:T(8,128)(2,1)} %plane_hbm.1) | copy-start | bytes 1228804
  4.4 0.9 %copy-start.4 = (bf16[1,1,320,320]{3,2,1,0:T(8,128)(2,1)S(1)}, bf16[1,1,320,320]{3,2,1,0:T(8,128)(2,1)}, u32[]{:S(2)}) copy-start(bf16[1,1,320,320]{3,2,1,0:T(8,128)(2,1)} %inverse_hbm.1) | copy-start | bytes 614404
  5.4 0.7 copy-start.5
